TPU v7x, 128 devices: a whole 4x4x4 slice. The times are simulated.
128 devices in a mesh: section: 8 (over x, y_lo), seq: 16 (over z, y_hi, core).
Axes of the slice: x: 4, y: 4 (y_hi: 2, y_lo: 2; y = y_hi * 2 + y_lo), z: 4, core: 2. Of those that a mesh axis runs over, the one named last changes fastest.
Arguments:
- inflow: bfloat16 [8, 1024, 4096], P('section', 'seq'), may hold values from -6 to 6
- fresh: bfloat16 [1, 1024, 4096], P(None, 'seq'), may hold values from -6 to 6
- proj_weight: bfloat16 [8, 4096, 640], P('section'), may hold values from -0.09375 to 0.09375
- xz_weight: bfloat16 [8, 4096, 2, 4096], P('section', None, None, 'seq'), may hold values from -0.09375 to 0.09375
- conv_weight: float32 [8, 4, 4608], P('section'), may hold values from -3 to 3
- conv_bias: float32 [8, 4608], P('section'), may hold values from -3 to 3
- step_bias: float32 [8, 128], P('section'), may hold values from -3 to 0
- decay_log: float32 [8, 128], P('section'), may hold values from -7 to -1
- skip_weight: float32 [8, 128], P('section'), may hold values from 0.5 to 1.5
- norm_gain: float32 [8, 4096], P('section'), may hold values from 0.5 to 1.5
- out_weight: bfloat16 [8, 4096, 4096], P('section', 'seq'), may hold values from -0.09375 to 0.09375
Outputs:
- section_outputs: float32 [8, 2, 1024, 4096], P('section', None, 'seq')
All inputs are finite; a program needn't handle non-finite values.
Results may differ from a plain program's by a relative error of at most 0.014.
Values may be sent and summed in bfloat16 or wider, within the bound.
A program may use at most 128 MiB of HBM per device.

v0:
```python
import functools

import jax
import jax.numpy as jnp
from jax import lax
from jax.experimental import pallas as pl
from jax.experimental.pallas import tpu as pltpu
from jax.sharding import PartitionSpec as P

MESH = pl.DeviceIdType.MESH
F32 = jnp.float32
BF16 = jnp.bfloat16
HIGHEST = lax.Precision.HIGHEST
TOKENS = 1024
WIDTH = 4096
CHAN = 256
BLOCK = 128
BLOCKS = TOKENS // BLOCK
ROWS = 64
HALF = WIDTH // 2
COLS = 896
TILES = ((0, 256), (256, 256), (512, 256), (768, 128))
LAST = 7
PAD = 16
COPIES = 192
MIB = 2**20


def aligned(value, by):
    return pl.multiple_of(value, by)


def iota(shape, dim):
    return lax.broadcasted_iota(jnp.int32, shape, dim)


def columns(p):
    return pl.ds(p * HALF, HALF)


def parts_of(value, count):
    parts = []
    for _ in range(count):
        part = value.astype(BF16)
        parts.append(part)
        value = value - part.astype(F32)
    return parts


class Place:
    def __init__(self):
        self.sec = lax.axis_index("section")
        self.me = lax.axis_index("seq")
        self.z, self.h, self.c = self.me // 4, (self.me // 2) % 2, self.me % 2
        self.zp, self.zm, self.zz = (self.z + 1) % 4, (self.z + 3) % 4, (self.z + 2) % 4
        self.hh = 1 - self.h
        self.up = self.device(self.zp, self.h, self.c)
        self.down = self.device(self.zm, self.h, self.c)
        self.across = self.device(self.z, self.hh, self.c)
        self.sib = self.device(self.z, self.h, 1 - self.c)
        self.diag = self.device(self.z, self.hh, 1 - self.c)
        self.after = ((self.sec + 1) % 8, self.me)
        self.ahead = ((self.sec + 7) % 8, self.me)

    def device(self, z, h, c):
        return (self.sec, z * 4 + h * 2 + c)

    def meet(self):
        targets = [self.up, self.down, self.across, self.sib, self.diag, self.after, self.ahead]
        barrier = pltpu.get_barrier_semaphore()
        for target in targets:
            pl.semaphore_signal(barrier, inc=1, device_id=target, device_id_type=MESH)
        pl.semaphore_wait(barrier, len(targets))


class Copies:
    def __init__(self, send_sem, recv_sem):
        self.send_sem, self.recv_sem = send_sem, recv_sem
        self.count = 0
        self.open = []

    def make(self, src, dst, target):
        index = self.count
        self.count += 1
        return pltpu.make_async_remote_copy(
            src_ref=src,
            dst_ref=dst,
            send_sem=self.send_sem.at[index],
            recv_sem=self.recv_sem.at[index],
            device_id=target,
            device_id_type=MESH,
        )

    def new(self, src, dst, target):
        copy = self.make(src, dst, target)
        copy.start()
        self.open.append(copy)
        return copy

    def finish(self):
        for copy in self.open:
            copy.wait_send()
        self.open = []


class Gather:
    def __init__(self, at, copies, source, act, weight, acc, proj):
        self.at, self.copies, self.source = at, copies, source
        self.act, self.weight, self.acc, self.proj = act, weight, acc, proj
        self.got = {}

    def rows(self, z, h, p, half=None):
        start = (z * 2 + h) * 128 + self.at.c * ROWS
        if half is None:
            return self.act.at[pl.ds(aligned(start, ROWS), ROWS), columns(p)]
        return self.act.at[pl.ds(aligned(start + half * 32, 32), 32), columns(p)]

    def forward(self, z, h, p, target, half=None):
        return self.copies.new(self.rows(z, h, p, half), self.rows(z, h, p, half), target)

    def share(self, name, z, h, p, half=None):
        self.got.setdefault((name, p), []).append(self.forward(z, h, p, self.at.sib, half))

    def own(self, p):
        at = self.at
        src = self.source.at[:, columns(p)]
        dst = self.rows(at.z, at.h, p)
        for name, target in (("up", at.up), ("down", at.down), ("across", at.across), ("own", at.sib)):
            self.got[name, p] = [self.copies.new(src, dst, target)]

    def arrived(self, name, p):
        for copy in self.got[name, p]:
            copy.wait_recv()

    def near(self, p):
        at = self.at
        self.arrived("up", p)
        self.got["cu", p] = [self.forward(at.zm, at.h, p, at.up, 0)]
        self.arrived("down", p)
        self.got["cd", p] = [self.forward(at.zp, at.h, p, at.down, 1)]
        self.share("s_zm", at.zm, at.h, p)
        self.share("s_zp", at.zp, at.h, p)
        self.arrived("across", p)
        self.got["pu", p] = [self.forward(at.z, at.hh, p, at.up)]
        self.got["pd", p] = [self.forward(at.z, at.hh, p, at.down)]
        self.share("s_p", at.z, at.hh, p)

    def far(self, p):
        at = self.at
        for name, half in (("cu", 0), ("cd", 1)):
            self.arrived(name, p)
            self.got["cy%d" % half, p] = [self.forward(at.zz, at.h, p, at.across, half)]
            self.share("s_c", at.zz, at.h, p, half)

    def beside(self, p):
        at = self.at
        self.arrived("pu", p)
        self.share("s_pm", at.zm, at.hh, p)
        self.arrived("pd", p)
        self.share("s_pp", at.zp, at.hh, p)

    def last(self, p):
        at = self.at
        for half in (0, 1):
            self.arrived("cy%d" % half, p)
            self.share("s_cy", at.zz, at.hh, p, half)

    def project(self, name, z, h, p):
        self.arrived(name, p)
        start = (z * 2 + h) * 128
        at = pl.ds(aligned(start, 128), 128)
        padded = pl.ds(aligned(start + PAD, PAD), 128)
        for first, size in TILES:
            cols = pl.ds(first, size)
            part = jnp.dot(
                self.act[at, columns(p)], self.weight[columns(p), cols], preferred_element_type=F32
            )
            if p == 0:
                self.acc[at, cols] = part
            else:
                self.proj[padded, cols] = (self.acc[at, cols] + part).astype(BF16)

    def project_near(self, p):
        at = self.at
        self.project("own", at.z, at.h, p)
        self.project("s_zm", at.zm, at.h, p)
        self.project("s_zp", at.zp, at.h, p)
        self.project("s_p", at.z, at.hh, p)

    def project_beside(self, p):
        at = self.at
        self.project("s_pm", at.zm, at.hh, p)
        self.project("s_pp", at.zp, at.hh, p)

    def rest(self, mixer, separate=None):
        at = self.at
        self.project_near(0)
        self.near(1)
        self.far(0)
        if separate is not None:
            separate(1)
        self.project_near(1)
        self.beside(0)
        self.project("s_c", at.zz, at.h, 0)
        self.far(1)
        mixer.local(0)
        self.project_beside(0)
        self.last(0)
        self.project("s_c", at.zz, at.h, 1)
        self.beside(1)
        self.project("s_cy", at.zz, at.hh, 0)
        self.project_beside(1)
        mixer.local(1)
        self.last(1)
        mixer.local(2)
        self.project("s_cy", at.zz, at.hh, 1)
        mixer.local(3)
        mixer.chain()


class Mixer:
    def __init__(self, at, params, proj, coded, sums, mixed, states, entering, window, gated, squares):
        self.proj, self.coded, self.sums, self.mixed = proj, coded, sums, mixed
        self.states, self.entering, self.window = states, entering, window
        self.gated, self.squares = gated, squares
        conv_w, conv_b, step_b, decay, skip, gain = params
        group = at.me // 4
        x_at = aligned(at.me * CHAN, CHAN)
        b_at = aligned(4096 + (group // 2) * 128, 128)
        c_at = aligned(4352 + (group // 2) * 128, 128)

        def own(ref):
            return jnp.concatenate(
                [ref[:, pl.ds(x_at, CHAN)], ref[:, pl.ds(b_at, 128)], ref[:, pl.ds(c_at, 128)]], axis=1
            )

        spread = (iota((128, CHAN), 0) == at.me * 8 + iota((128, CHAN), 1) // 32).astype(F32)

        def per_channel(ref):
            wide = jnp.broadcast_to(ref[...], (8, 128))
            return jnp.dot(wide, spread, precision=HIGHEST, preferred_element_type=F32)[0:1]

        self.taps, self.offset = own(conv_w), own(conv_b)
        self.bias = per_channel(step_b)
        self.rate = -jnp.exp(per_channel(decay))
        self.direct = per_channel(skip)
        self.gains = gain[:, pl.ds(x_at, CHAN)]
        self.spread = spread.astype(BF16)
        self.half = group % 2
        one, two = at.hh, at.h
        self.order = [
            one * (2 * at.z + 1) + two * (2 * at.z),
            one * (2 * at.zp) + two * (2 * at.z + 1),
            one * (2 * at.z) + two * (2 * at.zp),
            one * (2 * at.zm + 1) + two * (2 * at.zp + 1),
            one * (2 * at.zp + 1) + two * (2 * at.zm),
            one * (2 * at.zz) + two * (2 * at.zm + 1),
            one * (2 * at.zm) + two * (2 * at.zz),
            2 * at.zz + 1,
        ]
        proj[0:PAD, :] = jnp.zeros((PAD, COLS), BF16)

    def local(self, pair):
        first, second = self.order[2 * pair], self.order[2 * pair + 1]
        taps, window = self.taps, self.window
        lower = iota((BLOCK, BLOCK), 0) >= iota((BLOCK, BLOCK), 1)
        lower_ones = lower.astype(F32).astype(BF16)
        own_half = iota((BLOCK, 128), 1) // 64 == self.half
        head_of = iota((BLOCK, CHAN), 1) // 32

        def block(index, carry):
            start = ((1 - index) * first + index * second) * BLOCK
            at = pl.ds(aligned(start, BLOCK), BLOCK)
            rows = pl.ds(aligned(start + PAD, PAD), BLOCK)
            window[0:PAD, :] = self.proj[pl.ds(aligned(start, PAD), PAD), pl.ds(256, 512)].astype(F32)
            window[PAD : PAD + BLOCK, :] = self.proj[rows, pl.ds(256, 512)].astype(F32)
            conv = self.offset + taps[0:1] * window[PAD - 3 : PAD - 3 + BLOCK, :]
            for k in range(1, 4):
                conv = conv + taps[k : k + 1] * window[PAD - 3 + k : PAD - 3 + k + BLOCK, :]
            conv = (conv / (1.0 + jnp.exp(-conv))).astype(BF16)
            x = conv[:, :CHAN]
            b = conv[:, CHAN : CHAN + 128]
            c = jnp.where(own_half, conv[:, CHAN + 128 :], jnp.zeros((), BF16))
            self.coded[at, :] = c
            step = jax.nn.softplus(
                jnp.dot(self.proj[rows, pl.ds(768, 128)], self.spread, preferred_element_type=F32)
                + self.bias
            )
            cumulus = jnp.zeros((BLOCK, CHAN), F32)
            for part in parts_of(self.rate * step, 3):
                cumulus = cumulus + jnp.dot(lower_ones, part, preferred_element_type=F32)
            self.sums[at, :] = cumulus
            cumulus_t = cumulus.T
            step_t = step.T
            scores = lax.dot_general(c, b, (((1,), (1,)), ((), ())), preferred_element_type=F32)
            mixing, values = [], []
            for head in range(8):
                lane = 32 * head
                gap = cumulus[:, lane : lane + 1] - cumulus_t[lane : lane + 1, :]
                gap = jnp.where(lower, gap, -1e30)
                mixing.append((scores * jnp.exp(gap) * step_t[lane : lane + 1, :]).astype(BF16))
                values.append(jnp.where(head_of == head, x, jnp.zeros((), BF16)))
            diagonal = jnp.dot(
                jnp.concatenate(mixing, axis=1),
                jnp.concatenate(values, axis=0),
                preferred_element_type=F32,
            )
            x32 = x.astype(F32)
            self.mixed[at, :] = diagonal + self.direct * x32
            total = cumulus[BLOCK - 1 : BLOCK]
            weighted = (x32 * (jnp.exp(total - cumulus) * step)).astype(BF16)
            self.states[at, :] = lax.dot_general(
                b, weighted, (((0,), (0,)), ((), ())), preferred_element_type=F32
            )
            return carry

        lax.fori_loop(0, 2, block, 0)

    def chain(self):
        state = jnp.zeros((BLOCK, CHAN), F32)
        for index in range(BLOCKS):
            at = pl.ds(index * BLOCK, BLOCK)
            self.entering[at, :] = state.astype(BF16)
            if index < BLOCKS - 1:
                total = self.sums[(index + 1) * BLOCK - 1 : (index + 1) * BLOCK, :]
                state = jnp.exp(total) * state + self.states[at, :]

    def outputs(self, z):
        def block(index, carry):
            start = z * 256 + index * BLOCK
            at = pl.ds(aligned(start, BLOCK), BLOCK)
            mixed = self.mixed[at, :] + jnp.exp(self.sums[at, :]) * jnp.dot(
                self.coded[at, :], self.entering[at, :], preferred_element_type=F32
            )
            gate = self.proj[pl.ds(aligned(start + PAD, PAD), BLOCK), pl.ds(0, CHAN)].astype(F32)
            gated = mixed * (gate / (1.0 + jnp.exp(-gate)))
            total = jnp.zeros((8, BLOCK), F32)
            for part in parts_of(gated * gated, 2):
                total = total + lax.dot_general(
                    jnp.ones((8, CHAN), BF16), part, (((1,), (1,)), ((), ())), preferred_element_type=F32
                )
            self.squares[:, at] = total
            self.gated[at, :] = (gated * self.gains).astype(BF16)
            return carry

        lax.fori_loop(0, 2, block, 0)


class Scatter:
    def __init__(self, at, copies, mixer, wout, part, from_sib, got, stats, scale):
        self.at, self.copies, self.mixer, self.wout = at, copies, mixer, wout
        self.part, self.from_sib, self.got, self.stats, self.scale = part, from_sib, got, stats, scale
        self.sent = {}

    def gate(self, z):
        self.mixer.outputs(z)
        cols = pl.ds(aligned(z * 256, 256), 256)
        squares = self.mixer.squares.at[:, cols]
        self.shares = [
            self.copies.new(squares, self.stats.at[i, :, cols], target)
            for i, target in enumerate((self.at.sib, self.at.across, self.at.diag))
        ]
        return z, self.shares

    def factor(self, gate):
        z, shares = gate
        for share in shares:
            share.wait_recv()
        for i in (0, 1):
            at = pl.ds(aligned(z * 256 + i * 128, 128), 128)
            total = self.mixer.squares[:, at] + self.stats[0, :, at]
            total = total + self.stats[1, :, at] + self.stats[2, :, at]
            self.scale[at, :] = lax.dot_general(
                lax.rsqrt(total / 1024.0 + 1e-05),
                jnp.full((8, 128), 0.125, F32),
                (((0,), (0,)), ((), ())),
                precision=HIGHEST,
                preferred_element_type=F32,
            )

    def mine(self, z, h, p, half=None):
        start = (z * 2 + h) * 128 + self.at.c * ROWS
        if half is None:
            return self.part.at[pl.ds(aligned(start, ROWS), ROWS), columns(p)]
        return self.part.at[pl.ds(aligned(start + half * 32, 32), 32), columns(p)]

    def compute(self, z, p):
        at = pl.ds(aligned(z * 256, 256), 256)
        lhs = self.mixer.gated[at, :]

        def tile(n, carry):
            cols = pl.ds(aligned(p * HALF + n * 512, 512), 512)
            self.part[at, cols] = jnp.dot(
                lhs, self.wout[:, cols], preferred_element_type=F32
            ).astype(BF16)
            return carry

        lax.fori_loop(0, HALF // 512, tile, 0)
        copies = []
        for h in (self.at.hh, self.at.h):
            start = (z * 2 + h) * 128 + (1 - self.at.c) * ROWS
            src = self.part.at[pl.ds(aligned(start, ROWS), ROWS), columns(p)]
            dst = self.from_sib.at[pl.ds(aligned((z * 2 + h) * ROWS, ROWS), ROWS), columns(p)]
            copies.append(self.copies.new(src, dst, self.at.sib))
        return copies

    def pair(self, z, h, p, copy):
        copy.wait_recv()
        own = self.mine(z, h, p)
        other = self.from_sib.at[pl.ds(aligned((z * 2 + h) * ROWS, ROWS), ROWS), columns(p)]
        rows = pl.ds(aligned((z * 2 + h) * 128 + self.at.c * ROWS, ROWS), ROWS)
        scale = jnp.concatenate([self.scale[rows, :]] * 2, axis=1)

        def tile(n, carry):
            cols = pl.ds(aligned(n * 256, 256), 256)
            total = own[:, cols].astype(F32) + other[:, cols].astype(F32)
            own[:, cols] = (total * scale).astype(BF16)
            return carry

        lax.fori_loop(0, HALF // 256, tile, 0)

    @staticmethod
    def add(dst, *others):
        def tile(n, carry):
            cols = pl.ds(aligned(n * 256, 256), 256)
            total = dst[:, cols].astype(F32)
            for other in others:
                total = total + other[:, cols].astype(F32)
            dst[:, cols] = total.astype(BF16)
            return carry

        lax.fori_loop(0, HALF // 256, tile, 0)

    def send(self, name, src, slot, p, target, half=None):
        dst = self.got.at[p, slot]
        if half is not None:
            dst = self.got.at[p, slot, pl.ds(half * 32, 32)]
        self.sent.setdefault((name, p), []).append(self.copies.new(src, dst, target))

    def arrived(self, name, p):
        for copy in self.sent[name, p]:
            copy.wait_recv()

    def first(self):
        at = self.at
        g_zp = self.gate(at.zp)
        g_zm = self.gate(at.zm)
        zp_other, zp_own = self.compute(at.zp, 0)
        zm_other, zm_own = self.compute(at.zm, 0)
        g_zz = self.gate(at.zz)
        self.factor(g_zp)
        self.pair(at.zp, at.hh, 0, zp_other)
        self.send("u5", self.mine(at.zp, at.hh, 0), 1, 0, at.up)
        self.factor(g_zm)
        self.pair(at.zm, at.hh, 0, zm_other)
        self.send("d5", self.mine(at.zm, at.hh, 0), 2, 0, at.down)
        zz_other, zz_own = self.compute(at.zz, 0)
        g_z = self.gate(at.z)
        self.factor(g_zz)
        self.pair(at.zz, at.hh, 0, zz_other)
        self.send("y1", self.mine(at.zz, at.hh, 0), 0, 0, at.across)
        self.pair(at.zp, at.h, 0, zp_own)
        self.send("u4", self.mine(at.zp, at.h, 0, 0), 3, 0, at.up, 0)
        self.pair(at.zm, at.h, 0, zm_own)
        self.send("d4", self.mine(at.zm, at.h, 0, 1), 4, 0, at.down, 1)
        self.pair(at.zz, at.h, 0, zz_own)
        z_other, z_own = self.compute(at.z, 0)
        self.factor(g_z)
        self.pair(at.z, at.hh, 0, z_other)
        self.pair(at.z, at.h, 0, z_own)

    def second(self):
        at = self.at
        zp_other, zp_own = self.compute(at.zp, 1)
        zm_other, zm_own = self.compute(at.zm, 1)
        self.pair(at.zp, at.hh, 1, zp_other)
        self.pair(at.zm, at.hh, 1, zm_other)
        self.cross(0)
        self.side(0)
        self.send("u5", self.mine(at.zp, at.hh, 1), 1, 1, at.up)
        self.send("d5", self.mine(at.zm, at.hh, 1), 2, 1, at.down)
        zz_other, zz_own = self.compute(at.zz, 1)
        self.pair(at.zp, at.h, 1, zp_own)
        self.pair(at.zm, at.h, 1, zm_own)
        self.pair(at.zz, at.hh, 1, zz_other)
        self.send("y1", self.mine(at.zz, at.hh, 1), 0, 1, at.across)
        self.join(0)
        self.send("u4", self.mine(at.zp, at.h, 1, 0), 3, 1, at.up, 0)
        self.send("d4", self.mine(at.zm, at.h, 1, 1), 4, 1, at.down, 1)
        self.pair(at.zz, at.h, 1, zz_own)
        z_other, z_own = self.compute(at.z, 1)
        self.pair(at.z, at.hh, 1, z_other)
        self.pair(at.z, at.h, 1, z_own)

    def cross(self, p):
        at = self.at
        self.arrived("y1", p)
        self.add(self.mine(at.zz, at.h, p), self.got.at[p, 0])
        self.send("c_down", self.mine(at.zz, at.h, p, 0), 5, p, at.down, 0)
        self.send("c_up", self.mine(at.zz, at.h, p, 1), 5, p, at.up, 1)

    def side(self, p):
        at = self.at
        self.arrived("u5", p)
        self.arrived("d5", p)
        self.add(self.mine(at.z, at.hh, p), self.got.at[p, 1], self.got.at[p, 2])
        self.send("y6", self.mine(at.z, at.hh, p), 6, p, at.across)

    def join(self, p):
        at = self.at
        self.arrived("c_down", p)
        self.add(self.mine(at.zm, at.h, p, 0), self.got.at[p, 5, pl.ds(0, 32)])
        self.send("d4", self.mine(at.zm, at.h, p, 0), 4, p, at.down, 0)
        self.arrived("c_up", p)
        self.add(self.mine(at.zp, at.h, p, 1), self.got.at[p, 5, pl.ds(32, 32)])
        self.send("u4", self.mine(at.zp, at.h, p, 1), 3, p, at.up, 1)

    def total(self, p, out):
        at = self.at
        for name in ("y6", "u4", "d4"):
            self.arrived(name, p)
        own = self.mine(at.z, at.h, p)

        def tile(n, carry):
            cols = pl.ds(aligned(n * 256, 256), 256)
            wide = pl.ds(aligned(p * HALF + n * 256, 256), 256)
            total = own[:, cols].astype(F32) + self.got[p, 6, :, cols].astype(F32)
            total = total + self.got[p, 3, :, cols].astype(F32) + self.got[p, 4, :, cols].astype(F32)
            out[:, wide] = total.astype(BF16)
            return carry

        lax.fori_loop(0, HALF // 256, tile, 0)


def kernel(
    inflow, fresh, wxz, wproj, wout_hbm, conv_w, conv_b, step_b, decay, skip, gain, out,
    act, raw, wout, weight, acc, proj, coded, sums, mixed, states, entering, window, gated, squares,
    part, from_sib, got, stats, scale, received, send_sem, recv_sem, local_sem,
):
    at = Place()
    pair = at.z // 2
    here = pl.ds(aligned(at.me * ROWS, ROWS), ROWS)
    loads = []
    for index, (src, dst) in enumerate(
        [
            (inflow, act.at[here]),
            (wxz.at[pl.ds(0, HALF)], raw.at[pl.ds(0, HALF)]),
            (wxz.at[pl.ds(HALF, HALF)], raw.at[pl.ds(HALF, HALF)]),
            (wproj.at[:, pl.ds(aligned(pair * 128, 128), 128)], weight.at[:, pl.ds(512, 128)]),
            (wproj.at[:, pl.ds(aligned(256 + pair * 128, 128), 128)], weight.at[:, pl.ds(640, 128)]),
            (wproj.at[:, pl.ds(512, 128)], weight.at[:, pl.ds(768, 128)]),
            (wout_hbm, wout),
        ]
    ):
        load = pltpu.make_async_copy(src, dst, local_sem.at[index])
        load.start()
        loads.append(load)
    at.meet()
    copies = Copies(send_sem, recv_sem)
    mixer = Mixer(
        at, (conv_w, conv_b, step_b, decay, skip, gain),
        proj, coded, sums, mixed, states, entering, window, gated, squares,
    )
    scatter_refs = (wout, part, from_sib, got, stats, scale)

    gather = Gather(at, copies, inflow, act, weight, acc, proj)
    gather.own(0)
    gather.own(1)

    def separate(p):
        loads[1 + p].wait()

        def tile(n, carry):
            at = pl.ds(aligned(p * HALF + n * 128, 128), 128)
            weight[at, pl.ds(0, CHAN)] = raw[at, 0, :]
            weight[at, pl.ds(CHAN, CHAN)] = raw[at, 1, :]
            return carry

        lax.fori_loop(0, HALF // 128, tile, 0)

    separate(0)
    gather.near(0)
    for index in (0, 3, 4, 5):
        loads[index].wait()

    @pl.when(at.sec == 0)
    def _():
        load = pltpu.make_async_copy(fresh, received, local_sem.at[0])
        load.start()
        load.wait()

    gather.rest(mixer, separate)
    loads[6].wait()
    copies.finish()

    scatter = Scatter(at, copies, mixer, *scatter_refs)
    hops = [copies.make(out.at[0, :, columns(p)], received.at[:, columns(p)], at.after) for p in (0, 1)]

    def relay(p):
        scatter.total(p, out.at[0])
        pl.when(at.sec < LAST)(hops[p].start)

    def relayed(p):
        pl.when(at.sec > 0)(hops[p].wait_recv)
        keep = pltpu.make_async_copy(
            received.at[:, columns(p)], act.at[here, columns(p)], local_sem.at[p]
        )
        keep.start()
        gather.own(p)
        return keep

    scatter.first()
    scatter.second()
    relay(0)
    scatter.cross(1)
    scatter.side(1)
    scatter.join(1)
    gather = Gather(at, copies, received, act, weight, acc, proj)
    keeps = [relayed(0)]
    relay(1)
    gather.near(0)
    keeps.append(relayed(1))
    for keep in keeps:
        keep.wait()
    gather.rest(mixer)
    for p in (0, 1):
        pl.when(at.sec < LAST)(hops[p].wait_send)
    copies.finish()

    scatter = Scatter(at, copies, mixer, *scatter_refs)
    scatter.first()
    scatter.second()
    scatter.cross(1)
    scatter.side(1)
    scatter.total(0, out.at[1])
    scatter.join(1)
    scatter.total(1, out.at[1])
    copies.finish()


def on_device(
    inflow,
    fresh,
    proj_weight,
    xz_weight,
    conv_weight,
    conv_bias,
    step_bias,
    decay_log,
    skip_weight,
    norm_gain,
    out_weight,
):
    anywhere = pl.BlockSpec(memory_space=pl.ANY)
    vmem = pl.BlockSpec(memory_space=pltpu.VMEM)
    out = pl.pallas_call(
        kernel,
        out_shape=jax.ShapeDtypeStruct((2, ROWS, WIDTH), BF16),
        in_specs=[anywhere] * 5 + [vmem] * 6,
        out_specs=vmem,
        scratch_shapes=[
            pltpu.VMEM((TOKENS, WIDTH), BF16),
            pltpu.VMEM((WIDTH, 2, CHAN), BF16),
            pltpu.VMEM((CHAN, WIDTH), BF16),
            pltpu.VMEM((WIDTH, COLS), BF16),
            pltpu.VMEM((TOKENS, COLS), F32),
            pltpu.VMEM((TOKENS + PAD, COLS), BF16),
            pltpu.VMEM((TOKENS, 128), BF16),
            pltpu.VMEM((TOKENS, CHAN), F32),
            pltpu.VMEM((TOKENS, CHAN), F32),
            pltpu.VMEM((TOKENS, CHAN), F32),
            pltpu.VMEM((TOKENS, CHAN), BF16),
            pltpu.VMEM((BLOCK + PAD, 512), F32),
            pltpu.VMEM((TOKENS, CHAN), BF16),
            pltpu.VMEM((8, TOKENS), F32),
            pltpu.VMEM((TOKENS, WIDTH), BF16),
            pltpu.VMEM((TOKENS // 2, WIDTH), BF16),
            pltpu.VMEM((2, LAST, ROWS, HALF), BF16),
            pltpu.VMEM((3, 8, TOKENS), F32),
            pltpu.VMEM((TOKENS, 128), F32),
            pltpu.VMEM((ROWS, WIDTH), BF16),
            pltpu.SemaphoreType.DMA((COPIES,)),
            pltpu.SemaphoreType.DMA((COPIES,)),
            pltpu.SemaphoreType.DMA((7,)),
        ],
        compiler_params=pltpu.CompilerParams(
            collective_id=0, has_side_effects=True, vmem_limit_bytes=60 * MIB
        ),
        name="relay_window",
    )(
        inflow[0], fresh[0], xz_weight[0], proj_weight[0], out_weight[0],
        conv_weight[0], conv_bias, step_bias, decay_log, skip_weight, norm_gain,
    )
    return out.astype(F32)[None]


def solution(mesh):
    placed = (
        P("section", "seq", None),
        P(None, "seq", None),
        P("section", None, None),
        P("section", None, None, "seq"),
        P("section", None, None),
        P("section", None),
        P("section", None),
        P("section", None),
        P("section", None),
        P("section", None),
        P("section", "seq", None),
    )
    return jax.shard_map(
        on_device,
        mesh=mesh,
        in_specs=placed,
        out_specs=P("section", None, "seq", None),
        check_vma=False,
    )
```

profile of v0, /device:TPU:14, one launch (start us, length us, event | category | flops | bytes accessed | tf_op | source)
XLA Modules:
  0.0 179.4 jit_solution(14199731049729649329)
XLA Ops:
  0.0 176.7 %relay_window.1 = bf16[2,64,4096]{2,1,0:T(8,128)(2,1)} custom-call(bf16[64,4096]{1,0:T(8,128)(2,1)} %bitcast.12, bf16[64,4096]{1,0:T(8,128)(2,1)} %bitcast.13, bf16[4096,2,256]{2,1,0:T(2,128)(2,1)} %bitcast.10, bf16[4096,640]{1,0:T(8,128)(2,1)} %bitcast.9, bf16[256,4096]{1,0:T(8,128)(2,1)} %bitcast.11, f32[4,4608]{1,0:T(4,128)} %bitcast.14, ...), custom_call_target="tpu_custom_call" | custom-call | tf_op jit(solution)/shard_map/relay_window/pallas_call | solution.py:656
  176.7 2.8 %bitcast_convert_fusion = f32[1,2,64,4096]{3,2,1,0:T(8,128)} fusion(bf16[2,64,4096]{2,1,0:T(8,128)(2,1)} %relay_window.1), kind=kLoop, calls=%fused_computation | loop fusion | flops 524288 | bytes 3145728 | tf_op jit(solution)/shard_map/broadcast_in_dim | solution.py:694
where the time goes:
time: 180 us; the launch traced here: 179 us
  Pallas kernels  177 us (98%)
  other arithmetic  2.76 us (2%)
    pallas_call x1, Pallas kernels, on_device(): pl.pallas_call(kernel, out_shape=jax.ShapeDtypeStruct((2, ROWS, WIDTH), B...  177 us

commit v1 on v0

--- a/solution.py
+++ b/solution.py
@@ -343,7 +343,7 @@
             self.gated[at, :] = (gated * self.gains).astype(BF16)
             return carry
 
-        lax.fori_loop(0, 2, block, 0)
+        lax.fori_loop(0, 2, block, 0, unroll=True)
 
 
 class Scatter:

time: 180 us -> 180 us (level)
  no operation moved by 1% of the time
where the time goes in v1:
time: 180 us; the launch traced here: 179 us
  Pallas kernels  177 us (98%)
  other arithmetic  2.76 us (2%)
    pallas_call x1, Pallas kernels, on_device(): pl.pallas_call(kernel, out_shape=jax.ShapeDtypeStruct((2, ROWS, WIDTH), B...  177 us

profile of v1, /device:TPU:14, one launch (start us, length us, event | category | flops | bytes accessed | tf_op | source)
XLA Modules:
  0.0 179.5 jit_solution(3700560110716834905)
XLA Ops:
  0.0 176.7 %relay_window.1 = bf16[2,64,4096]{2,1,0:T(8,128)(2,1)} custom-call(bf16[64,4096]{1,0:T(8,128)(2,1)} %bitcast.12, bf16[64,4096]{1,0:T(8,128)(2,1)} %bitcast.13, bf16[4096,2,256]{2,1,0:T(2,128)(2,1)} %bitcast.10, bf16[4096,640]{1,0:T(8,128)(2,1)} %bitcast.9, bf16[256,4096]{1,0:T(8,128)(2,1)} %bitcast.11, f32[4,4608]{1,0:T(4,128)} %bitcast.14, ...), custom_call_target="tpu_custom_call" | custom-call | tf_op jit(solution)/shard_map/relay_window/pallas_call | solution.py:656
  176.7 2.8 %bitcast_convert_fusion = f32[1,2,64,4096]{3,2,1,0:T(8,128)} fusion(bf16[2,64,4096]{2,1,0:T(8,128)(2,1)} %relay_window.1), kind=kLoop, calls=%fused_computation | loop fusion | flops 524288 | bytes 3145728 | tf_op jit(solution)/shard_map/broadcast_in_dim | solution.py:694
